TPU v7x, 512 devices: a whole 4x4x16 slice. The times are simulated.
512 devices in a mesh: node: 32 (over x, y, core), local: 16 (over z).
Axes of the slice: x: 4, y: 4, z: 16, core: 2. Of those that a mesh axis runs over, the one named last changes fastest.
Arguments:
- tokens: bfloat16 [2048, 6144], P('node', 'local'), may hold values from -6 to 6
- cotangent: bfloat16 [2048, 6144], P('node', 'local'), may hold values from -6 to 6
- node_list: int32 [2048, 4], P('node'), may hold values from 0 to 31, as said below
- expert_ids: int32 [2048, 6], P('node'), may hold values from 0 to 63, as said below
- gate_ints: int32 [2048, 6], P('node'), may hold values from 1 to 1023
- w_gate: bfloat16 [6144, 65536], P(None, ('node', 'local')), may hold values from -0.078125 to 0.078125
- w_up: bfloat16 [6144, 65536], P(None, ('node', 'local')), may hold values from -0.078125 to 0.078125
- w_down: bfloat16 [65536, 6144], P('node', 'local'), may hold values from -0.1875 to 0.1875
Outputs:
- mixed: bfloat16 [2048, 6144], P('node', 'local')
- grad_tokens: bfloat16 [2048, 6144], P('node', 'local')
Inputs may be any that keep to these rules, and one draw needn't show every extreme that they name: `node_list`: A token's 4 node groups are distinct; the tokens of each node group name every node group exactly 8 times in all. `expert_ids`: A token's 6 experts are distinct, and each lies in one of the token's node groups (expert e lies in group e // 2).
All inputs are finite; a program needn't handle non-finite values.
Results may differ from a plain program's by a relative error of at most 0.034.
Values may be sent and summed in bfloat16 or wider, within the bound.
No kernel may reach another device: no remote copies, remote signals or barrier semaphores. Data moves between devices by JAX's collectives and lax.ppermute only.
A program may use at most 64 MiB of HBM per device.

v0:
```python
import jax
import jax.numpy as jnp
from jax import lax
from jax.sharding import PartitionSpec as P

EXP_NODE = 2


FIRST_DIMS = (((0,), (0,)), ((), ()))
FIRST_SECOND = (((0,), (1,)), ((), ()))
SECOND_DIMS = (((1,), (1,)), ((), ()))


def gather_back(received, position, tok_rows, per_token):
    feat_cols = received.shape[0]
    columns = received.reshape(feat_cols, -1)[:, position]
    summed = jnp.sum(columns.reshape(feat_cols, tok_rows, per_token), axis=2)
    return summed.T.astype(jnp.bfloat16)


def per_device(tokens, cotangent, node_list, expert_ids, gate_ints, w_gate, w_up, w_down):
    tok_rows, feat_cols = tokens.shape
    per_token = node_list.shape[1]
    node_count = lax.axis_size("node")
    local_count = lax.axis_size("local")
    flat_count = tok_rows * per_token
    node_cap = flat_count // node_count
    counts = gate_ints.astype(jnp.float32)
    weight_share = counts / jnp.sum(counts, axis=1, keepdims=True)
    within = jnp.arange(EXP_NODE, dtype=jnp.int32)
    candidate = node_list[:, :, None] * EXP_NODE + within[None, None, :]
    match_table = expert_ids[:, None, None, :] == candidate[:, :, :, None]
    picked = jnp.where(match_table, weight_share[:, None, None, :], 0.0)
    route_gate = jnp.sum(picked, axis=3).astype(jnp.bfloat16).reshape(flat_count, EXP_NODE)
    node_flat = node_list.reshape(flat_count)
    onehot = (node_flat[:, None] == jnp.arange(node_count, dtype=jnp.int32)[None, :]).astype(
        jnp.int32
    )
    slot_index = jnp.sum((jnp.cumsum(onehot, axis=0) - onehot) * onehot, axis=1)
    position = node_flat * node_cap + slot_index
    source_of = (
        jnp.zeros((flat_count,), jnp.int32)
        .at[position]
        .set(jnp.arange(flat_count, dtype=jnp.int32))
    )
    token_of = source_of // per_token
    send_gate = route_gate[source_of].reshape(node_count, node_cap, EXP_NODE)
    send_grad = cotangent[token_of].reshape(node_count, node_cap, feat_cols)
    send_rows = tokens[token_of].reshape(node_count, node_cap, feat_cols)
    got_rows, got_gate, got_grad = (
        lax.all_to_all(send_rows, "node", split_axis=0, concat_axis=0, tiled=True),
        lax.all_to_all(send_gate, "node", split_axis=0, concat_axis=0, tiled=True),
        lax.all_to_all(send_grad, "node", split_axis=0, concat_axis=0, tiled=True),
    )
    rows_in = got_rows.reshape(flat_count, feat_cols)
    portion = lax.all_gather(rows_in, "local", axis=1, tiled=True)
    gate_piece = w_gate
    up_piece = w_up
    gate_sum = lax.dot_general(
        gate_piece, portion, FIRST_SECOND, preferred_element_type=jnp.float32
    )
    up_sum = lax.dot_general(up_piece, portion, FIRST_SECOND, preferred_element_type=jnp.float32)
    own_expert = lax.axis_index("local") // (local_count // EXP_NODE)
    gates_in = got_gate.reshape(flat_count, EXP_NODE).astype(jnp.float32)
    own_gate = jnp.sum(jnp.where(within[None, :] == own_expert, gates_in, 0.0), axis=1)[None, :]
    sigmoid_gate = jax.nn.sigmoid(gate_sum)
    swish = gate_sum * sigmoid_gate
    activation = (swish * up_sum * own_gate).astype(jnp.bfloat16)
    down_piece = w_down
    out_cols = lax.dot_general(
        down_piece,
        lax.all_gather(activation, "local", axis=0, tiled=True),
        FIRST_DIMS,
        preferred_element_type=jnp.float32,
    )
    back_out = lax.all_to_all(
        out_cols.reshape(feat_cols, node_count, node_cap).astype(jnp.bfloat16),
        "node",
        split_axis=1,
        concat_axis=1,
        tiled=True,
    ).astype(jnp.float32)
    grads_in = got_grad.reshape(flat_count, feat_cols)
    down_piece = w_down
    grad_act = lax.psum_scatter(
        lax.dot_general(
            down_piece, grads_in, SECOND_DIMS, preferred_element_type=jnp.float32
        ).astype(jnp.bfloat16),
        "local",
        scatter_dimension=0,
        tiled=True,
    ).astype(jnp.float32)
    grad_up = (grad_act * own_gate * swish).astype(jnp.bfloat16)
    grad_pre = (
        grad_act * own_gate * up_sum * sigmoid_gate * (1.0 + gate_sum * (1.0 - sigmoid_gate))
    ).astype(jnp.bfloat16)
    gate_piece = w_gate
    up_piece = w_up
    partial_value = jnp.dot(gate_piece, grad_pre, preferred_element_type=jnp.float32)
    grad_cols = lax.psum_scatter(
        (partial_value + jnp.dot(up_piece, grad_up, preferred_element_type=jnp.float32)).astype(
            jnp.bfloat16
        ),
        "local",
        scatter_dimension=0,
        tiled=True,
    ).astype(jnp.float32)
    back_grad = lax.all_to_all(
        grad_cols.reshape(feat_cols, node_count, node_cap).astype(jnp.bfloat16),
        "node",
        split_axis=1,
        concat_axis=1,
        tiled=True,
    ).astype(jnp.float32)
    mixed_out = gather_back(back_out, position, tok_rows, per_token)
    grad_out = gather_back(back_grad, position, tok_rows, per_token)
    return (mixed_out, grad_out)


def solution(mesh):
    in_specs = (
        P("node", "local"),
        P("node", "local"),
        P("node", None),
        P("node", None),
        P("node", None),
        P(None, ("node", "local")),
        P(None, ("node", "local")),
        P("node", "local"),
    )
    out_specs = (P("node", "local"), P("node", "local"))
    return jax.shard_map(
        per_device, mesh=mesh, in_specs=in_specs, out_specs=out_specs, check_vma=False
    )
```

profile of v0, /device:TPU:1, one launch (start us, length us, event | category | flops | bytes accessed | tf_op | source)
XLA Modules:
  0.0 351.1 jit_solution(13998908110377946967)
XLA Ops:
  7.2 0.8 broadcast_multiply_fusion
  8.0 0.8 copy.29
  10.2 1.4 scatter_custom_fusion
  11.6 2.0 gather_fusion
  13.6 18.8 %all_to_all.25 = bf16[32,8,384]{2,1,0:T(8,128)(2,1)} all-to-all(bf16[32,8,384]{2,1,0:T(8,128)(2,1)S(1)} %bitcast.76), channel_id=1, replica_groups=mesh['node'=32,'local'=16] {'node'}, dimensions={0} | all-to-all | bytes 393216 | tf_op jit(solution)/shard_map/all_to_all | solution.py:51
  32.4 1.2 gather_fusion.3
  33.6 11.9 %all_to_all.26 = bf16[32,8,384]{2,1,0:T(8,128)(2,1)S(1)} all-to-all(bf16[32,8,384]{2,1,0:T(8,128)(2,1)S(1)} %bitcast.75), channel_id=1, replica_groups=mesh['node'=32,'local'=16] {'node'}, dimensions={0} | all-to-all | bytes 393216 | tf_op jit(solution)/shard_map/all_to_all | solution.py:53
  45.4 1.7 fusion.2
  47.2 2.4 copy.34
  49.8 0.9 gather_fusion.1
  50.7 0.9 copy.33
  51.6 3.7 %all-to-all-start.1 = ((bf16[32,8,2]{1,2,0:T(2,128)(2,1)}), bf16[32,8,2]{1,2,0:T(2,128)(2,1)S(1)}, u32[]{:S(2)}, u32[]{:S(2)}) async-start(bf16[32,8,2]{1,2,0:T(2,128)(2,1)} %copy.33), calls=%async_computation.1 | async-start | bytes 32768 | tf_op jit(solution)/shard_map/all_to_all | solution.py:52
  55.4 6.9 %all-to-all-done.1 = bf16[32,8,2]{1,2,0:T(2,128)(2,1)S(1)} async-done(((bf16[32,8,2]{1,2,0:T(2,128)(2,1)}), bf16[32,8,2]{1,2,0:T(2,128)(2,1)S(1)}, u32[]{:S(2)}, u32[]{:S(2)}) %all-to-all-start.1) | async-done | bytes 1056 | tf_op jit(solution)/shard_map/all_to_all | solution.py:52
  62.5 36.6 %all-gather.3.cloned.1.call-done = bf16[256,6144]{1,0:T(8,128)(2,1)} async-done(((bf16[256,384]{1,0:T(8,128)(2,1)}), bf16[256,6144]{1,0:T(8,128)(2,1)}) %all-gather.3.cloned.1.call-update) | async-done | bytes 3145744 | tf_op jit(solution)/shard_map/all_gather | solution.py:56
  99.1 3.0 convolution_bitcast_fusion.1
  102.2 1.7 multiply_convert_fusion.2
  103.9 63.4 %reduce-scatter.7.cloned.1.call-done = bf16[128,256]{1,0:T(8,128)(2,1)} async-done(((bf16[2048,256]{1,0:T(8,128)(2,1)}), bf16[128,256]{1,0:T(8,128)(2,1)}) %reduce-scatter.7.cloned.1.call-update) | async-done | bytes 65552
  167.3 0.9 copy.35
  168.2 1.0 fusion.6
  169.2 2.7 fusion.1
  172.0 4.6 %copy.36 = bf16[6144,256]{1,0:T(8,128)(2,1)} copy(bf16[6144,256]{0,1:T(8,128)(2,1)} %fusion.1) | data formatting | bytes 6291456
  176.7 61.6 %all-gather.5.cloned.1.call-done = bf16[2048,256]{0,1:T(8,128)(2,1)} async-done(((bf16[128,256]{0,1:T(8,128)(2,1)}), bf16[2048,256]{0,1:T(8,128)(2,1)}) %all-gather.5.cloned.1.call-update) | async-done | bytes 1048592 | tf_op jit(solution)/shard_map/all_gather | solution.py:72
  238.3 2.6 fusion.3
  240.9 18.7 %all-to-all-start.2 = ((bf16[384,32,8]{0,2,1:T(8,128)(2,1)}), bf16[384,32,8]{0,2,1:T(8,128)(2,1)S(1)}, u32[]{:S(2)}, u32[]{:S(2)}) async-start(bf16[384,32,8]{0,2,1:T(8,128)(2,1)} %fusion.3), calls=%async_computation.2 | async-start | bytes 393216 | tf_op jit(solution)/shard_map/all_to_all | solution.py:76
  259.6 56.0 %reduce-scatter.9.cloned.1.call-done = bf16[384,256]{1,0:T(8,128)(2,1)} async-done(((bf16[6144,256]{1,0:T(8,128)(2,1)}), bf16[384,256]{1,0:T(8,128)(2,1)}) %reduce-scatter.9.cloned.1.call-update) | async-done | bytes 196624
  315.6 1.7 copy.37
  317.3 16.9 %all-to-all-start.4 = ((bf16[384,32,8]{0,2,1:T(8,128)(2,1)}), bf16[384,32,8]{0,2,1:T(8,128)(2,1)S(1)}, u32[]{:S(2)}, u32[]{:S(2)}) async-start(bf16[384,32,8]{0,2,1:T(8,128)(2,1)} %bitcast.18), calls=%async_computation.4 | async-start | bytes 393216 | tf_op jit(solution)/shard_map/all_to_all | solution.py:108
  334.3 1.0 gather_fusion.2
  335.4 0.9 reduce_sum.61
  336.3 6.3 %all-to-all-done.4 = bf16[384,32,8]{0,2,1:T(8,128)(2,1)S(1)} async-done(((bf16[384,32,8]{0,2,1:T(8,128)(2,1)}), bf16[384,32,8]{0,2,1:T(8,128)(2,1)S(1)}, u32[]{:S(2)}, u32[]{:S(2)}) %all-to-all-start.4) | async-done | bytes 196640 | tf_op jit(solution)/shard_map/all_to_all | solution.py:108
  342.6 1.0 gather_fusion.4
  343.7 0.9 reduce_sum.62
  (52 shorter events, 2.3 us)
Async XLA Ops:
  7.2 95.0 %copy-start = (bf16[6144,128]{1,0:T(8,128)(2,1)S(1)}, bf16[6144,128]{1,0:T(8,128)(2,1)}, u32[]{:S(2)}) copy-start(bf16[6144,128]{1,0:T(8,128)(2,1)} %param.14) | copy-start | bytes 4718596
  7.2 25.2 %copy-start.1 = (bf16[64,384]{1,0:T(8,128)(2,1)S(1)}, bf16[64,384]{1,0:T(8,128)(2,1)}, u32[]{:S(2)}) copy-start(bf16[64,384]{1,0:T(8,128)(2,1)} %param.9) | copy-start | bytes 147460
  7.2 91.9 %all-gather.3.cloned.1.call-start = ((), (), s32[]{:S(2)}) async-start(), calls=%async_computation.7 | async-start | bytes 3342336 | tf_op jit(solution)/shard_map/all_gather | solution.py:56
  13.6 31.9 %copy-start.4 = (bf16[2048,384]{1,0:T(8,128)(2,1)S(1)}, bf16[2048,384]{1,0:T(8,128)(2,1)}, u32[]{:S(2)}) copy-start(bf16[2048,384]{1,0:T(8,128)(2,1)} %param.15) | copy-start | bytes 4718596
  32.4 134.9 %reduce-scatter.7.cloned.1.call-start = ((), (), s32[]{:S(2)}) async-start(), calls=%async_computation.9 | async-start | bytes 1114112
  47.2 2.4 copy-start.6
  47.2 2.5 copy-start.7
  47.2 51.9 %copy-start.2 = (bf16[6144,128]{1,0:T(8,128)(2,1)S(1)}, bf16[6144,128]{1,0:T(8,128)(2,1)}, u32[]{:S(2)}) copy-start(bf16[6144,128]{1,0:T(8,128)(2,1)} %param.13) | copy-start | bytes 4718596
  51.6 10.7 %all-to-all-start.1 = ((bf16[32,8,2]{1,2,0:T(2,128)(2,1)}), bf16[32,8,2]{1,2,0:T(2,128)(2,1)S(1)}, u32[]{:S(2)}, u32[]{:S(2)}) async-start(bf16[32,8,2]{1,2,0:T(2,128)(2,1)} %copy.33), calls=%async_computation.1 | async-start | bytes 32768 | tf_op jit(solution)/shard_map/all_to_all | solution.py:52
  55.3 183.0 %all-gather.5.cloned.1.call-start = ((), (), s32[]{:S(2)}) async-start(), calls=%async_computation.8 | async-start | bytes 1114112 | tf_op jit(solution)/shard_map/all_gather | solution.py:72
  99.1 3.0 copy-start.3
  103.8 211.7 %reduce-scatter.9.cloned.1.call-start = ((), (), s32[]{:S(2)}) async-start(), calls=%async_computation.10 | async-start | bytes 3342336
  176.6 61.7 %copy-start.5 = (bf16[2048,384]{1,0:T(8,128)(2,1)S(1)}, bf16[2048,384]{1,0:T(8,128)(2,1)}, u32[]{:S(2)}) copy-start(bf16[2048,384]{1,0:T(8,128)(2,1)} %param.15) | copy-start | bytes 4718596
  240.9 76.4 %all-to-all-start.2 = ((bf16[384,32,8]{0,2,1:T(8,128)(2,1)}), bf16[384,32,8]{0,2,1:T(8,128)(2,1)S(1)}, u32[]{:S(2)}, u32[]{:S(2)}) async-start(bf16[384,32,8]{0,2,1:T(8,128)(2,1)} %fusion.3), calls=%async_computation.2 | async-start | bytes 393216 | tf_op jit(solution)/shard_map/all_to_all | solution.py:76
  317.3 25.2 %all-to-all-start.4 = ((bf16[384,32,8]{0,2,1:T(8,128)(2,1)}), bf16[384,32,8]{0,2,1:T(8,128)(2,1)S(1)}, u32[]{:S(2)}, u32[]{:S(2)}) async-start(bf16[384,32,8]{0,2,1:T(8,128)(2,1)} %bitcast.18), calls=%async_computation.4 | async-start | bytes 393216 | tf_op jit(solution)/shard_map/all_to_all | solution.py:108
Sparse Core Ops, SparseCore 0:
  32.5 66.5 all-gather.2
  101.9 65.2 reduce-scatter.6
  169.5 68.7 all-gather.4
  241.2 74.3 reduce-scatter.8
where the time goes:
time: 352 us; the launch traced here: 351 us
  waiting for transfers between devices  231 us (66%)
  starting transfers between devices  39.5 us (11%)
  blocking collectives  30.6 us (9%)
  local copies, waits for them, and re-layouts  19.8 us (6%)
  between operations  14 us (4%)
  matrix products  12.8 us (4%)
    unnamed x6, waiting for transfers between devices  119 us
    all_gather x1, waiting for transfers between devices, per_device(): lax.all_gather(activation, 'local', axis=0, tiled=True)  61.6 us
    all_gather x1, waiting for transfers between devices, per_device(): portion = lax.all_gather(rows_in, 'local', axis=1, tiled=True)  36.6 us
    all_to_all x1, blocking collectives, per_device(): lax.all_to_all(send_rows, 'node', split_axis=0, concat_axis=0, tiled=True)  18.8 us
    all_to_all x1, starting transfers between devices, per_device(): lax.all_to_all(out_cols.reshape(feat_cols, node_count, node_cap).astype(j...  18.7 us
    all_to_all x1, starting transfers between devices, per_device(): lax.all_to_all(grad_cols.reshape(feat_cols, node_count, node_cap).astype(...  16.9 us
    all_to_all x1, blocking collectives, per_device(): lax.all_to_all(send_grad, 'node', split_axis=0, concat_axis=0, tiled=True)  11.9 us
    unnamed x21, local copies, waits for them, and re-layouts  10.5 us
  transfers between devices with their start and end apart: 7, of which 6 were waited for; matrix products, arithmetic and copies ran while one was open for 8% of the time, Pallas kernels for 0%

commit v1 on v0

v1 whole, which is shorter than its diff:
```python
import functools

import jax
import jax.numpy as jnp
from jax import lax
from jax.experimental import pallas as pl
from jax.experimental.pallas import tpu as pltpu
from jax.sharding import PartitionSpec as P

EXP_NODE = 2
F32 = jnp.float32
BF16 = jnp.bfloat16
NT = (((1,), (1,)), ((), ()))
TN = (((0,), (0,)), ((), ()))
NN = (((1,), (0,)), ((), ()))


def dot(a, b, dims=NN):
    return lax.dot_general(a, b, dims, preferred_element_type=F32)


def kernel_call(body, outs, args, flops, in_specs=None):
    moved = sum(a.size * a.dtype.itemsize for a in args)
    moved += sum(o.size * o.dtype.itemsize for o in outs)
    vmem = pl.BlockSpec(memory_space=pltpu.VMEM)
    return pl.pallas_call(
        body,
        out_shape=outs,
        in_specs=in_specs or [vmem] * len(args),
        out_specs=[vmem] * len(outs),
        compiler_params=pltpu.CompilerParams(vmem_limit_bytes=32 * 1024 * 1024),
        cost_estimate=pl.CostEstimate(flops=flops, bytes_accessed=moved, transcendentals=0),
    )(*args)


def shape(dims, dtype=BF16):
    return jax.ShapeDtypeStruct(dims, dtype)


def route_body(cap, own_ref, nodes_ref, experts_ref, counts_ref, cot_ref, place_ref, send_ref):
    slots, toks = place_ref.shape
    feat = cot_ref.shape[1]
    slot = lax.broadcasted_iota(jnp.int32, (slots, toks), 0)
    group = slot // cap
    within = slot - group * cap
    named = jnp.zeros((slots, toks), F32)
    for j in range(nodes_ref.shape[0]):
        named = jnp.where(nodes_ref[j : j + 1, :] == group, 1.0, named)
    before = lax.broadcasted_iota(jnp.int32, (toks, toks), 0)
    after = lax.broadcasted_iota(jnp.int32, (toks, toks), 1)
    earlier = jnp.where(before < after, 1.0, 0.0).astype(BF16)
    rank = dot(named.astype(BF16), earlier)
    place = jnp.where(rank == within.astype(F32), named, 0.0)
    place_ref[...] = place.astype(BF16)
    counts = counts_ref[...].astype(F32)
    share = counts / jnp.sum(counts, axis=0, keepdims=True)
    expert = group * EXP_NODE + own_ref[0]
    picked = jnp.zeros((slots, toks), F32)
    for k in range(experts_ref.shape[0]):
        picked = picked + jnp.where(experts_ref[k : k + 1, :] == expert, share[k : k + 1, :], 0.0)
    gate = jnp.sum(picked * place, axis=1, keepdims=True)
    send_ref[:, :feat] = dot(place.astype(BF16), cot_ref[...]).astype(BF16)
    send_ref[:, feat:] = jnp.broadcast_to(gate, (slots, send_ref.shape[1] - feat)).astype(BF16)


def spread_body(order, feat, place_ref, full_ref, send_ref):
    for index, z in enumerate(order):
        rows = dot(place_ref[...], full_ref[index])
        send_ref[:, z * feat : (z + 1) * feat] = rows.astype(BF16)


def act_grad_body(feat, got_ref, down_ref, out_ref):
    hidden = out_ref.shape[2]
    for z in range(out_ref.shape[0]):
        out_ref[z] = dot(got_ref[:, :feat], down_ref[z * hidden : (z + 1) * hidden, :], NT).astype(BF16)


def up_body(feat, rows_ref, gate_w_ref, up_w_ref, got_ref, act_ref, pre_gate_ref, pre_up_ref):
    pre_gate = dot(rows_ref[...], gate_w_ref[...])
    pre_up = dot(rows_ref[...], up_w_ref[...])
    gate = got_ref[:, feat:].astype(F32)
    act_ref[...] = (pre_gate * jax.nn.sigmoid(pre_gate) * pre_up * gate).astype(BF16)
    pre_gate_ref[...] = pre_gate
    pre_up_ref[...] = pre_up


def row_grad_body(feat, grad_ref, pre_gate_ref, pre_up_ref, got_ref, gate_w_ref, up_w_ref, out_ref):
    pre_gate = pre_gate_ref[...]
    sig = jax.nn.sigmoid(pre_gate)
    scaled = grad_ref[...].astype(F32) * got_ref[:, feat:].astype(F32)
    grad_up = (scaled * (pre_gate * sig)).astype(BF16)
    grad_pre = (scaled * pre_up_ref[...] * sig * (1.0 + pre_gate * (1.0 - sig))).astype(BF16)
    for z in range(out_ref.shape[0]):
        cols = slice(z * feat, (z + 1) * feat)
        part = dot(grad_pre, gate_w_ref[cols, :], NT) + dot(grad_up, up_w_ref[cols, :], NT)
        out_ref[z] = part.astype(BF16)


def down_body(order, act_ref, down_ref, out_ref):
    hidden = act_ref.shape[2]
    total = jnp.zeros(out_ref.shape, F32)
    for index, z in enumerate(order):
        total = total + dot(act_ref[index], down_ref[z * hidden : (z + 1) * hidden, :])
    out_ref[...] = total.astype(BF16)


def combine_body(place_ref, back_ref, out_ref):
    out_ref[...] = dot(place_ref[...], back_ref[...], TN).astype(BF16)


def per_device(tokens, cotangent, node_list, expert_ids, gate_ints, w_gate, w_up, w_down):
    toks, feat = tokens.shape
    width, hidden = w_gate.shape
    nodes = lax.axis_size("node")
    local = lax.axis_size("local")
    slots = toks * node_list.shape[1]
    cap = slots // nodes
    low = 4
    high = local // low
    far_groups = [[low * b + a for b in range(high)] for a in range(low)]
    near_groups = [[low * a + b for b in range(low)] for a in range(high)]
    order = [low * b + a for a in range(low) for b in range(high)]
    extra = 128

    def swap_nodes(value):
        cut = value.reshape(nodes, cap, value.shape[1])
        moved = lax.all_to_all(cut, "node", split_axis=0, concat_axis=0, tiled=True)
        return moved.reshape(value.shape)

    own = (lax.axis_index("local") // (local // EXP_NODE)).astype(jnp.int32).reshape(1)
    smem = pl.BlockSpec(memory_space=pltpu.SMEM)
    vmem = pl.BlockSpec(memory_space=pltpu.VMEM)
    place, send = kernel_call(
        functools.partial(route_body, cap),
        [shape((slots, toks)), shape((slots, feat + extra))],
        [own, node_list.T, expert_ids.T, gate_ints.T, cotangent],
        2 * slots * toks * (toks + feat),
        in_specs=[smem] + [vmem] * 4,
    )
    got = swap_nodes(send)
    (act_grad_parts,) = kernel_call(
        functools.partial(act_grad_body, feat),
        [shape((local, slots, hidden))],
        [got, w_down],
        2 * slots * feat * local * hidden,
    )
    far = lax.all_gather(tokens, "local", axis=0, tiled=False, axis_index_groups=far_groups)
    far, act_grad_parts = lax.optimization_barrier((far, act_grad_parts))
    far = far.reshape(high * toks, feat)
    act_grad = lax.psum_scatter(act_grad_parts, "local", scatter_dimension=0, tiled=False)
    full = lax.all_gather(far, "local", axis=0, tiled=False, axis_index_groups=near_groups)
    full = full.reshape(local, toks, feat)
    (send_rows,) = kernel_call(
        functools.partial(spread_body, order, feat),
        [shape((slots, width))],
        [place, full],
        2 * slots * toks * width,
    )
    rows = swap_nodes(send_rows)
    act, pre_gate, pre_up = kernel_call(
        functools.partial(up_body, feat),
        [shape((slots, hidden)), shape((slots, hidden), F32), shape((slots, hidden), F32)],
        [rows, w_gate, w_up, got],
        4 * slots * width * hidden,
    )
    (grad_parts,) = kernel_call(
        functools.partial(row_grad_body, feat),
        [shape((local, slots, feat))],
        [act_grad, pre_gate, pre_up, got, w_gate, w_up],
        4 * slots * width * hidden,
    )
    row_grad = lax.psum_scatter(grad_parts, "local", scatter_dimension=0, tiled=False)

    far_act = lax.all_gather(act, "local", axis=0, tiled=False, axis_index_groups=far_groups)
    copies = jnp.broadcast_to(far_act[None], (low,) + far_act.shape)
    full_act = lax.all_to_all(
        copies, "local", split_axis=0, concat_axis=0, tiled=True, axis_index_groups=near_groups
    ).reshape(local, slots, hidden)
    (out_rows,) = kernel_call(
        functools.partial(down_body, order),
        [shape((slots, feat))],
        [full_act, w_down],
        2 * slots * feat * local * hidden,
    )
    combine = functools.partial(
        kernel_call, combine_body, [shape((toks, feat))], flops=2 * slots * toks * feat
    )
    (mixed,) = combine([place, swap_nodes(out_rows)])
    (grad_tokens,) = combine([place, swap_nodes(row_grad)])
    return mixed, grad_tokens


def solution(mesh):
    in_specs = (
        P("node", "local"),
        P("node", "local"),
        P("node", None),
        P("node", None),
        P("node", None),
        P(None, ("node", "local")),
        P(None, ("node", "local")),
        P("node", "local"),
    )
    out_specs = (P("node", "local"), P("node", "local"))
    return jax.shard_map(
        per_device, mesh=mesh, in_specs=in_specs, out_specs=out_specs, check_vma=False
    )
```

time: 352 us -> 265 us (0.75)
  waiting for transfers between devices: 231 us -> 67.4 us
  blocking collectives: 30.6 us -> 117 us
  matrix products: 12.8 us -> 0 us
  Pallas kernels: 0 us -> 10.8 us
    unnamed x6 -> x2, waiting for transfers between devices: 119 us -> 0.7 us
    all_gather x2 -> x0, waiting for transfers between devices: 98.3 us -> none  [the longest x1 61.6 us: per_device(): lax.all_gather(activation, 'local', axis=0, tiled=True)]
    all_gather x0 -> x3, blocking collectives: none -> 54.9 us  [the longest x1 21.8 us: per_device(): lax.all_gather(tokens, 'local', axis=0, tiled=False, axis_index_groups=fa...]
    all_to_all x3, waiting for transfers between devices: 13.2 us -> 46.5 us  [swap_nodes(): moved = lax.all_to_all(cut, 'node', split_axis=0, concat_axis=0, tiled=True)]
    all_to_all x2, blocking collectives: 30.6 us -> 61.9 us  [the longest x1 34.3 us: per_device(): lax.all_to_all(copies, 'local', split_axis=0, concat_axis=0, tiled=True,...]
    reduce_scatter x0 -> x2, waiting for transfers between devices: none -> 20.2 us  [the longest x1 14.2 us: per_device(): lax.psum_scatter(act_grad_parts, 'local', scatter_dimension=0, tiled=False)]
    dot_general x6 -> x0, matrix products: 12.8 us -> none  [the longest x1 3 us: per_device(): lax.dot_general(gate_piece, portion, FIRST_SECOND, preferred_element_type...]
    pallas_call x0 -> x8, Pallas kernels: none -> 10.8 us  [kernel_call(): pl.pallas_call(body, out_shape=outs, in_specs=in_specs or [vmem] * len(ar...]
  transfers between devices with their start and end apart: 7 -> 5, of which waited for: 6 -> 4; matrix products, arithmetic and copies ran while one was open for 8% -> 0% of each run, Pallas kernels for 0% -> 1%
where the time goes in v1:
time: 265 us; the launch traced here: 264 us
  blocking collectives  117 us (44%)
  waiting for transfers between devices  67.4 us (25%)
  starting transfers between devices  38.2 us (14%)
  local copies, waits for them, and re-layouts  16.6 us (6%)
  between operations  14.2 us (5%)
  Pallas kernels  10.8 us (4%)
    all_to_all x3, waiting for transfers between devices, swap_nodes(): moved = lax.all_to_all(cut, 'node', split_axis=0, concat_axis=0, tiled=True)  46.5 us
    all_to_all x3, starting transfers between devices, swap_nodes(): moved = lax.all_to_all(cut, 'node', split_axis=0, concat_axis=0, tiled=True)  38.2 us
    all_to_all x1, blocking collectives, per_device(): lax.all_to_all(copies, 'local', split_axis=0, concat_axis=0, tiled=True,...  34.3 us
    all_to_all x1, blocking collectives, swap_nodes(): moved = lax.all_to_all(cut, 'node', split_axis=0, concat_axis=0, tiled=True)  27.6 us
    all_gather x1, blocking collectives, per_device(): lax.all_gather(tokens, 'local', axis=0, tiled=False, axis_index_groups=fa...  21.8 us
    all_gather x1, blocking collectives, per_device(): lax.all_gather(act, 'local', axis=0, tiled=False, axis_index_groups=far_g...  18.7 us
    unnamed x34, local copies, waits for them, and re-layouts  16.4 us
    all_gather x1, blocking collectives, per_device(): lax.all_gather(far, 'local', axis=0, tiled=False, axis_index_groups=near_...  14.4 us
  transfers between devices with their start and end apart: 5, of which 4 were waited for; matrix products, arithmetic and copies ran while one was open for 0% of the time, Pallas kernels for 1%

profile of v1, /device:TPU:1, one launch (start us, length us, event | category | flops | bytes accessed | tf_op | source)
XLA Modules:
  0.0 264.0 jit_solution(15263808729285325501)
XLA Ops:
  7.2 0.8 copy-done.13
  8.0 0.7 copy-done.14
  10.0 1.0 shard_map.95
  11.1 10.4 %all-to-all-start = ((bf16[32,8,512]{2,1,0:T(8,128)(2,1)}), bf16[32,8,512]{2,1,0:T(8,128)(2,1)S(1)}, u32[]{:S(2)}, u32[]{:S(2)}) async-start(bf16[32,8,512]{2,1,0:T(8,128)(2,1)} %bitcast.5), calls=%async_computation | async-start | bytes 524288 | tf_op jit(solution)/shard_map/all_to_all | solution.py:127
  21.5 21.8 %all-gather = bf16[256,384]{1,0:T(8,128)(2,1)S(1)} all-gather(bf16[64,384]{1,0:T(8,128)(2,1)} %param.8), channel_id=2, replica_groups={{0,4,8,12},{1,5,9,13},{2,6,10,14},{3,7,11,15},{16,20,24,28},{17,21,25,2..., dimensions={0}, use_global_device_ids=true | all-gather | bytes 245760 | tf_op jit(solution)/shard_map/all_gather | solution.py:147
  43.2 1.4 copy-done.5
  44.6 1.0 shard_map.96
  45.6 1.0 copy-done.7
  46.6 14.4 %all_gather.17 = bf16[4,256,384]{2,1,0:T(8,128)(2,1)S(1)} all-gather(bf16[1,256,384]{2,1,0:T(8,128)(2,1)S(1)} %bitcast.33), channel_id=1, replica_groups={{0,1,2,3},{4,5,6,7},{8,9,10,11},{12,13,14,15},{16,17,18,19},{20,21,22,2..., dimensions={0}, use_global_device_ids=true | all-gather | bytes 983040 | tf_op jit(solution)/shard_map/all_gather | solution.py:151
  61.0 1.0 shard_map.97
  62.0 1.6 copy-done
  63.6 13.9 %all-to-all-start.1 = ((bf16[32,8,6144]{2,1,0:T(8,128)(2,1)}), bf16[32,8,6144]{2,1,0:T(8,128)(2,1)S(1)}, u32[]{:S(2)}, u32[]{:S(2)}) async-start(bf16[32,8,6144]{2,1,0:T(8,128)(2,1)} %bitcast.19), calls=%async_computation.1 | async-start | bytes 6291456 | tf_op jit(solution)/shard_map/all_to_all | solution.py:127
  78.3 39.0 %all-to-all-done.1 = bf16[32,8,6144]{2,1,0:T(8,128)(2,1)S(1)} async-done(((bf16[32,8,6144]{2,1,0:T(8,128)(2,1)}), bf16[32,8,6144]{2,1,0:T(8,128)(2,1)S(1)}, u32[]{:S(2)}, u32[]{:S(2)}) %all-to-all-start.1) | async-done | bytes 3145760 | tf_op jit(solution)/shard_map/all_to_all | solution.py:127
  117.3 1.4 copy-done.1
  118.7 1.4 copy-done.3
  120.1 1.8 shard_map.98
  123.2 14.2 %reduce-scatter.3.cloned.1.call-done = bf16[1,256,128]{2,1,0:T(8,128)(2,1)} async-done(((bf16[16,256,128]{2,1,0:T(8,128)(2,1)}), bf16[1,256,128]{2,1,0:T(8,128)(2,1)}) %reduce-scatter.3.cloned.1.call-update) | async-done | bytes 65552 | tf_op jit(solution)/shard_map/reduce_scatter | solution.py:150
  137.4 1.4 copy-done.2
  138.8 1.4 copy-done.4
  140.3 0.9 copy-done.9
  141.2 0.9 copy-done.11
  142.1 0.8 copy-done.12
  142.9 3.4 %shard_map.101 = bf16[16,256,384]{2,1,0:T(8,128)(2,1)} custom-call(bf16[256,128]{1,0:T(8,128)(2,1)S(1)} %bitcast.28, f32[256,128]{1,0:T(8,128)S(1)} %copy-done.9, f32[256,128]{1,0:T(8,128)S(1)} %copy-done.11, bf16[256,512]{1,0:T(8,128)(2,1)S(1)} %bitcast.23, bf16[6144,128]{1,0:T(8,128)(2,1)S(1)} %copy-done.2, bf16[6144,128]{1,0:T(8,128)(2,1)S(1)} %copy-done.4), custom_call_target="tpu_custom_call" | custom-call | flops 805306368 | bytes 6881280 | tf_op jit(solution)/shard_map/pallas_call | solution.py:26
  146.4 18.7 %all-gather.1 = bf16[1024,128]{1,0:T(8,128)(2,1)S(1)} all-gather(bf16[256,128]{1,0:T(8,128)(2,1)S(1)} %get-tuple-element.12), channel_id=3, replica_groups={{0,4,8,12},{1,5,9,13},{2,6,10,14},{3,7,11,15},{16,20,24,28},{17,21,25,2..., dimensions={0}, use_global_device_ids=true | all-gather | bytes 327680 | tf_op jit(solution)/shard_map/all_gather | solution.py:174
  165.3 34.3 %all_to_all.25 = bf16[4,4,256,128]{3,2,1,0:T(8,128)(2,1)S(1)} all-to-all(bf16[4,4,256,128]{3,2,1,0:T(8,128)(2,1)S(1)} %broadcast_in_dim.2), channel_id=1, replica_groups={{0,1,2,3},{4,5,6,7},{8,9,10,11},{12,13,14,15},{16,17,18,19},{20,21,22,2..., dimensions={0} | all-to-all | bytes 2097152 | tf_op jit(solution)/shard_map/all_to_all | solution.py:176
  199.6 1.0 shard_map.99
  200.6 27.6 %all_to_all.26 = bf16[32,8,384]{2,1,0:T(8,128)(2,1)S(1)} all-to-all(bf16[32,8,384]{2,1,0:T(8,128)(2,1)S(1)} %bitcast.27), channel_id=1, replica_groups=mesh['node'=32,'local'=16] {'node'}, dimensions={0} | all-to-all | bytes 393216 | tf_op jit(solution)/shard_map/all_to_all | solution.py:127
  228.2 5.9 %reduce-scatter.5.cloned.1.call-done = bf16[1,256,384]{2,1,0:T(8,128)(2,1)} async-done(((bf16[16,256,384]{2,1,0:T(8,128)(2,1)}), bf16[1,256,384]{2,1,0:T(8,128)(2,1)}) %reduce-scatter.5.cloned.1.call-update) | async-done | bytes 196624 | tf_op jit(solution)/shard_map/reduce_scatter | solution.py:172
  234.1 13.8 %all-to-all-start.4 = ((bf16[32,8,384]{2,1,0:T(8,128)(2,1)}), bf16[32,8,384]{2,1,0:T(8,128)(2,1)S(1)}, u32[]{:S(2)}, u32[]{:S(2)}) async-start(bf16[32,8,384]{2,1,0:T(8,128)(2,1)} %bitcast.34), calls=%async_computation.6 | async-start | bytes 393216 | tf_op jit(solution)/shard_map/all_to_all | solution.py:127
  248.0 0.8 shard_map.100
  248.8 7.5 %all-to-all-done.4 = bf16[32,8,384]{2,1,0:T(8,128)(2,1)S(1)} async-done(((bf16[32,8,384]{2,1,0:T(8,128)(2,1)}), bf16[32,8,384]{2,1,0:T(8,128)(2,1)S(1)}, u32[]{:S(2)}, u32[]{:S(2)}) %all-to-all-start.4) | async-done | bytes 196640 | tf_op jit(solution)/shard_map/all_to_all | solution.py:127
  256.3 0.8 shard_map.102
  (28 shorter events, 3.7 us)
Async XLA Ops:
  7.2 0.8 copy-start.13
  8.0 0.7 copy-start.14
  8.7 0.7 copy-start.15
  9.4 0.7 copy-start.16
  11.1 32.2 %all-to-all-start = ((bf16[32,8,512]{2,1,0:T(8,128)(2,1)}), bf16[32,8,512]{2,1,0:T(8,128)(2,1)S(1)}, u32[]{:S(2)}, u32[]{:S(2)}) async-start(bf16[32,8,512]{2,1,0:T(8,128)(2,1)} %bitcast.5), calls=%async_computation | async-start | bytes 524288 | tf_op jit(solution)/shard_map/all_to_all | solution.py:127
  43.2 1.4 copy-start.5
  45.6 1.0 copy-start.7
  62.0 1.6 copy-start
  63.6 53.7 %all-to-all-start.1 = ((bf16[32,8,6144]{2,1,0:T(8,128)(2,1)}), bf16[32,8,6144]{2,1,0:T(8,128)(2,1)S(1)}, u32[]{:S(2)}, u32[]{:S(2)}) async-start(bf16[32,8,6144]{2,1,0:T(8,128)(2,1)} %bitcast.19), calls=%async_computation.1 | async-start | bytes 6291456 | tf_op jit(solution)/shard_map/all_to_all | solution.py:127
  77.5 59.9 %reduce-scatter.3.cloned.1.call-start = ((), (), s32[]{:S(2)}) async-start(), calls=%async_computation.7 | async-start | bytes 1114112 | tf_op jit(solution)/shard_map/reduce_scatter | solution.py:150
  78.2 155.9 %reduce-scatter.5.cloned.1.call-start = ((), (), s32[]{:S(2)}) async-start(), calls=%async_computation.8 | async-start | bytes 3342336 | tf_op jit(solution)/shard_map/reduce_scatter | solution.py:172
  117.3 1.4 copy-start.1
  118.7 1.4 copy-start.3
  121.9 0.6 copy-start.8
  122.5 0.7 copy-start.10
  137.4 1.4 copy-start.2
  138.8 1.4 copy-start.4
  140.3 0.9 copy-start.9
  141.2 0.9 copy-start.11
  142.1 0.8 copy-start.12
  146.3 53.3 %copy-start.6 = (bf16[2048,384]{1,0:T(8,128)(2,1)S(1)}, bf16[2048,384]{1,0:T(8,128)(2,1)}, u32[]{:S(2)}) copy-start(bf16[2048,384]{1,0:T(8,128)(2,1)} %down_ref.3) | copy-start | bytes 4718596
  234.1 22.2 %all-to-all-start.4 = ((bf16[32,8,384]{2,1,0:T(8,128)(2,1)}), bf16[32,8,384]{2,1,0:T(8,128)(2,1)S(1)}, u32[]{:S(2)}, u32[]{:S(2)}) async-start(bf16[32,8,384]{2,1,0:T(8,128)(2,1)} %bitcast.34), calls=%async_computation.6 | async-start | bytes 393216 | tf_op jit(solution)/shard_map/all_to_all | solution.py:127
Sparse Core Ops, SparseCore 0:
  81.1 56.2 reduce-scatter.2
  146.5 87.5 reduce-scatter.4

commit v2 on v1

v2 whole, which is shorter than its diff:
```python
import functools

import jax
import jax.numpy as jnp
from jax import lax
from jax.experimental import pallas as pl
from jax.experimental.pallas import tpu as pltpu
from jax.sharding import PartitionSpec as P

EXP_NODE = 2
F32 = jnp.float32
BF16 = jnp.bfloat16
NT = (((1,), (1,)), ((), ()))
TN = (((0,), (0,)), ((), ()))
NN = (((1,), (0,)), ((), ()))


def dot(a, b, dims=NN):
    return lax.dot_general(a, b, dims, preferred_element_type=F32)


def kernel_call(body, outs, args, flops, fetch=(), scalars=(), unread=(), vmem_mib=32):
    moved = sum(a.size * a.dtype.itemsize for a in args)
    moved += sum(o.size * o.dtype.itemsize for o in outs)
    vmem = pl.BlockSpec(memory_space=pltpu.VMEM)
    specs = [vmem] * len(args)
    for index in (*fetch, *unread):
        specs[index] = pl.BlockSpec(memory_space=pl.ANY)
    for index in scalars:
        specs[index] = pl.BlockSpec(memory_space=pltpu.SMEM)
    scratch = [pltpu.VMEM(args[index].shape, args[index].dtype) for index in fetch]
    if fetch:
        scratch.append(pltpu.SemaphoreType.DMA((len(fetch),)))

    def whole(*refs):
        refs = list(refs)
        count = len(args) + len(outs)
        copies = []
        for number, index in enumerate(fetch):
            copies.append(
                pltpu.make_async_copy(refs[index], refs[count + number], refs[-1].at[number])
            )
            refs[index] = refs[count + number]
        for copy in copies:
            copy.start()
        for copy in copies:
            copy.wait()
        body(*refs[:count])

    return pl.pallas_call(
        whole,
        out_shape=outs,
        in_specs=specs,
        out_specs=[vmem] * len(outs),
        scratch_shapes=scratch,
        compiler_params=pltpu.CompilerParams(vmem_limit_bytes=vmem_mib * 1024 * 1024),
        cost_estimate=pl.CostEstimate(flops=flops, bytes_accessed=moved, transcendentals=0),
        name=body.func.__name__ if isinstance(body, functools.partial) else body.__name__,
    )(*args)


def shape(dims, dtype=BF16):
    return jax.ShapeDtypeStruct(dims, dtype)


def route_body(cap, own_ref, nodes_ref, experts_ref, counts_ref, cot_ref, place_ref, send_ref):
    slots, toks = place_ref.shape
    feat = cot_ref.shape[1]
    slot = lax.broadcasted_iota(jnp.int32, (slots, toks), 0)
    group = slot // cap
    within = slot - group * cap
    named = jnp.zeros((slots, toks), F32)
    for j in range(nodes_ref.shape[0]):
        named = jnp.where(nodes_ref[j : j + 1, :] == group, 1.0, named)
    before = lax.broadcasted_iota(jnp.int32, (toks, toks), 0)
    after = lax.broadcasted_iota(jnp.int32, (toks, toks), 1)
    earlier = jnp.where(before < after, 1.0, 0.0).astype(BF16)
    rank = dot(named.astype(BF16), earlier)
    place = jnp.where(rank == within.astype(F32), named, 0.0)
    place_ref[...] = place.astype(BF16)
    counts = counts_ref[...].astype(F32)
    share = counts / jnp.sum(counts, axis=0, keepdims=True)
    expert = group * EXP_NODE + own_ref[0]
    picked = jnp.zeros((slots, toks), F32)
    for k in range(experts_ref.shape[0]):
        picked = picked + jnp.where(experts_ref[k : k + 1, :] == expert, share[k : k + 1, :], 0.0)
    gate = jnp.sum(picked * place, axis=1, keepdims=True)
    send_ref[:, :feat] = dot(place.astype(BF16), cot_ref[...]).astype(BF16)
    send_ref[:, feat:] = jnp.broadcast_to(gate, (slots, send_ref.shape[1] - feat)).astype(BF16)


def spread_body(order, feat, place_ref, full_ref, send_ref):
    for index, z in enumerate(order):
        rows = dot(place_ref[...], full_ref[index])
        send_ref[:, z * feat : (z + 1) * feat] = rows.astype(BF16)


def act_grad_body(order, feat, got_ref, down_ref, out_ref):
    hidden = out_ref.shape[2]
    for index, z in enumerate(order):
        rows = slice(z * hidden, (z + 1) * hidden)
        out_ref[index] = dot(got_ref[:, :feat], down_ref[rows, :], NT).astype(BF16)


def near_sum_body(high_ref, parts_ref, *out_refs):
    high = len(out_refs)
    for step in range(high):
        block = lax.rem(high_ref[0] + step, high)
        total = parts_ref[0, block].astype(F32)
        for sender in range(1, parts_ref.shape[0]):
            total = total + parts_ref[sender, block].astype(F32)
        out_refs[step][...] = total.astype(BF16)


def add_body(*refs):
    total = refs[0][...].astype(F32)
    for ref in refs[1:-1]:
        total = total + ref[...].astype(F32)
    refs[-1][...] = total.astype(refs[-1].dtype)


def expert_body(feat, rows_ref, gate_w_ref, up_w_ref, got_ref, grad_ref, act_ref, out_ref):
    pre_gate = dot(rows_ref[...], gate_w_ref[...])
    pre_up = dot(rows_ref[...], up_w_ref[...])
    gate = got_ref[:, feat:].astype(F32)
    sig = jax.nn.sigmoid(pre_gate)
    gated = pre_gate * sig * gate
    act_ref[...] = (gated * pre_up).astype(BF16)
    grad = grad_ref[...]
    grad_up = (grad * gated).astype(BF16)
    grad_pre = (grad * (gate * pre_up * sig * (1.0 + pre_gate * (1.0 - sig)))).astype(BF16)
    for start in range(0, out_ref.shape[1], feat):
        cols = slice(start, start + feat)
        part = dot(grad_pre, gate_w_ref[cols, :], NT) + dot(grad_up, up_w_ref[cols, :], NT)
        out_ref[:, cols] = part.astype(BF16)


def down_body(parts, *refs):
    act_refs, down_ref, out_ref = refs[:parts], refs[-2], refs[-1]
    total = jnp.zeros(out_ref.shape, F32)
    first = 0
    for act_ref in act_refs:
        low, high, _, hidden = act_ref.shape
        for b in range(high):
            for a in range(0, low, 2):
                z = low * (first + b) + a
                act = jnp.concatenate([act_ref[a, b], act_ref[a + 1, b]], axis=1)
                total = total + dot(act, down_ref[z * hidden : (z + 2) * hidden, :])
        first += high
    out_ref[...] = total.astype(BF16)


def combine_body(place_ref, back_ref, out_ref):
    out_ref[...] = dot(place_ref[...], back_ref[...], TN).astype(BF16)


def combine_parts_body(order, feat, place_ref, back_ref, out_ref):
    for index, z in enumerate(order):
        cols = slice(z * feat, (z + 1) * feat)
        out_ref[index] = dot(place_ref[...], back_ref[:, cols], TN).astype(BF16)


def per_device(tokens, cotangent, node_list, expert_ids, gate_ints, w_gate, w_up, w_down):
    toks, feat = tokens.shape
    width, hidden = w_gate.shape
    nodes = lax.axis_size("node")
    local = lax.axis_size("local")
    slots = toks * node_list.shape[1]
    cap = slots // nodes
    low = 4
    high = local // low
    far_groups = [[low * b + a for b in range(high)] for a in range(low)]
    near_groups = [[low * a + b for b in range(low)] for a in range(high)]
    order = [low * b + a for a in range(low) for b in range(high)]
    extra = 128

    def swap_nodes(value):
        cut = value.reshape(nodes, cap, value.shape[1])
        moved = lax.all_to_all(cut, "node", split_axis=0, concat_axis=0, tiled=True)
        return moved.reshape(value.shape)

    own = (lax.axis_index("local") // (local // EXP_NODE)).astype(jnp.int32).reshape(1)
    place, send = kernel_call(
        functools.partial(route_body, cap),
        [shape((slots, toks)), shape((slots, feat + extra))],
        [own, node_list.T, expert_ids.T, gate_ints.T, cotangent],
        2 * slots * toks * (toks + feat),
        fetch=(1, 2, 3, 4),
        scalars=(0,),
        vmem_mib=63,
    )
    got = swap_nodes(send)
    (act_grad_parts,) = kernel_call(
        functools.partial(act_grad_body, order, feat),
        [shape((local, slots, hidden))],
        [got, w_down],
        2 * slots * feat * local * hidden,
    )

    own_high = (lax.axis_index("local") // low).astype(jnp.int32).reshape(1)

    def swap_near(parts):
        count, rows, cols = parts.shape
        moved = lax.all_to_all(
            parts.reshape(low, high * rows, cols),
            "local",
            split_axis=0,
            concat_axis=0,
            tiled=True,
            axis_index_groups=near_groups,
        )
        return kernel_call(
            near_sum_body,
            [shape((rows, cols))] * high,
            [own_high, moved.reshape(low, high, rows, cols)],
            count * rows * cols,
            scalars=(0,),
        )

    def swap_far(sums):
        moved = [sums[0]]
        for step in range(1, high):
            pairs = [(z, (z + step * low) % local) for z in range(local)]
            moved.append(lax.ppermute(sums[step], "local", pairs))
        return moved

    def gather(value, groups):
        return lax.all_gather(value, "local", axis=0, tiled=True, axis_index_groups=groups)

    far = gather(tokens, far_groups)
    far, act_grad_parts = lax.optimization_barrier((far, act_grad_parts))
    act_grads = swap_far(swap_near(act_grad_parts))
    (act_grad,) = kernel_call(
        add_body, [shape((slots, hidden), F32)], act_grads, high * slots * hidden
    )
    full = gather(far, near_groups).reshape(local, toks, feat)
    (send_rows,) = kernel_call(
        functools.partial(spread_body, order, feat),
        [shape((slots, width))],
        [place, full],
        2 * slots * toks * width,
    )
    rows = swap_nodes(send_rows)
    act, grad_parts = kernel_call(
        functools.partial(expert_body, feat),
        [shape((slots, hidden)), shape((slots, width))],
        [rows, w_gate, w_up, got, act_grad],
        8 * slots * width * hidden,
    )

    far_act = gather(act, far_groups)
    first_act, last_act = far_act[: high // 2 * slots], far_act[high // 2 * slots :]
    first_act = gather(first_act, near_groups)
    back_parts = swap_nodes(grad_parts)
    first_act, back_parts = lax.optimization_barrier((first_act, back_parts))
    (own_parts,) = kernel_call(
        functools.partial(combine_parts_body, order, feat),
        [shape((local, toks, feat))],
        [place, back_parts],
        2 * slots * toks * width,
    )
    last_act, own_parts = lax.optimization_barrier((last_act, own_parts))
    near_sums = swap_near(own_parts)
    last_act = gather(last_act, near_groups)
    (out_rows,) = kernel_call(
        functools.partial(down_body, 2),
        [shape((slots, feat))],
        [part.reshape(low, high // 2, slots, hidden) for part in (first_act, last_act)] + [w_down],
        2 * slots * feat * local * hidden,
    )
    near_sums, out_rows = lax.optimization_barrier((near_sums, out_rows))
    far_sums = swap_far(near_sums)
    (mixed,) = kernel_call(
        combine_body, [shape((toks, feat))], [place, swap_nodes(out_rows)], 2 * slots * toks * feat
    )
    (grad_tokens,) = kernel_call(
        add_body, [shape((toks, feat))], far_sums, high * toks * feat
    )
    return mixed, grad_tokens


def solution(mesh):
    in_specs = (
        P("node", "local"),
        P("node", "local"),
        P("node", None),
        P("node", None),
        P("node", None),
        P(None, ("node", "local")),
        P(None, ("node", "local")),
        P("node", "local"),
    )
    out_specs = (P("node", "local"), P("node", "local"))
    return jax.shard_map(
        per_device, mesh=mesh, in_specs=in_specs, out_specs=out_specs, check_vma=False
    )
```

time: 265 us -> 257 us (0.970)
  starting transfers between devices: 38.2 us -> 74.2 us
  waiting for transfers between devices: 67.4 us -> 36.4 us
  between operations: 14.2 us -> 0.87 us
  local copies, waits for them, and re-layouts: 16.6 us -> 13.8 us
    all_gather x3 -> x5, blocking collectives: 54.9 us -> 119 us  [gather(): lax.all_gather(value, 'local', axis=0, tiled=True, axis_index_groups=groups)]
    all_to_all x2 -> x0, blocking collectives: 61.9 us -> none  [the longest x1 34.3 us: per_device(): lax.all_to_all(copies, 'local', split_axis=0, concat_axis=0, tiled=True,...]
    ppermute x0 -> x6, starting transfers between devices: none -> 32.3 us  [swap_far(): moved.append(lax.ppermute(sums[step], 'local', pairs))]
    all_to_all x3 -> x4, waiting for transfers between devices: 46.5 us -> 17.9 us  [swap_nodes(): moved = lax.all_to_all(cut, 'node', split_axis=0, concat_axis=0, tiled=True)]
    reduce_scatter x2 -> x0, waiting for transfers between devices: 20.2 us -> none  [the longest x1 14.2 us: per_device(): lax.psum_scatter(act_grad_parts, 'local', scatter_dimension=0, tiled=False)]
    ppermute x0 -> x6, waiting for transfers between devices: none -> 18.5 us  [swap_far(): moved.append(lax.ppermute(sums[step], 'local', pairs))]
    all_to_all x0 -> x2, starting transfers between devices: none -> 7.39 us  [swap_near(): lax.all_to_all(parts.reshape(low, high * rows, cols), 'local', split_axis...]
    all_to_all x3 -> x4, starting transfers between devices: 38.2 us -> 34.5 us  [swap_nodes(): moved = lax.all_to_all(cut, 'node', split_axis=0, concat_axis=0, tiled=True)]
  transfers between devices with their start and end apart: 5 -> 12, of which waited for: 4 -> 6; matrix products, arithmetic and copies ran while one was open for 0% -> 0% of each run, Pallas kernels for 1% -> 1%
where the time goes in v2:
time: 257 us; the launch traced here: 256 us
  blocking collectives  119 us (46%)
  starting transfers between devices  74.2 us (29%)
  waiting for transfers between devices  36.4 us (14%)
  local copies, waits for them, and re-layouts  13.8 us (5%)
  Pallas kernels  12 us (5%)
    all_gather x5, blocking collectives, gather(): lax.all_gather(value, 'local', axis=0, tiled=True, axis_index_groups=groups)  119 us
    all_to_all x4, starting transfers between devices, swap_nodes(): moved = lax.all_to_all(cut, 'node', split_axis=0, concat_axis=0, tiled=True)  34.5 us
    ppermute x6, starting transfers between devices, swap_far(): moved.append(lax.ppermute(sums[step], 'local', pairs))  32.3 us
    ppermute x6, waiting for transfers between devices, swap_far(): moved.append(lax.ppermute(sums[step], 'local', pairs))  18.5 us
    all_to_all x4, waiting for transfers between devices, swap_nodes(): moved = lax.all_to_all(cut, 'node', split_axis=0, concat_axis=0, tiled=True)  17.9 us
    unnamed x28, local copies, waits for them, and re-layouts  13.2 us
    pallas_call x11, Pallas kernels, kernel_call(): pl.pallas_call(whole, out_shape=outs, in_specs=specs, out_specs=[vmem] *...  12 us
    all_to_all x2, starting transfers between devices, swap_near(): lax.all_to_all(parts.reshape(low, high * rows, cols), 'local', split_axis...  7.39 us
  transfers between devices with their start and end apart: 12, of which 6 were waited for; matrix products, arithmetic and copies ran while one was open for 0% of the time, Pallas kernels for 1%

profile of v2, /device:TPU:1, one launch (start us, length us, event | category | flops | bytes accessed | tf_op | source)
XLA Modules:
  0.0 255.7 jit_solution(10001927646107792325)
XLA Ops:
  0.6 1.9 route_body.1
  2.6 10.4 %all-to-all-start = ((bf16[32,8,512]{2,1,0:T(8,128)(2,1)}), bf16[32,8,512]{2,1,0:T(8,128)(2,1)S(1)}, u32[]{:S(2)}, u32[]{:S(2)}) async-start(bf16[32,8,512]{2,1,0:T(8,128)(2,1)} %bitcast.33), calls=%async_computation | async-start | bytes 524288 | tf_op jit(solution)/shard_map/all_to_all | solution.py:179
  13.0 22.2 %all_gather.15 = bf16[256,384]{1,0:T(8,128)(2,1)S(1)} all-gather(bf16[64,384]{1,0:T(8,128)(2,1)} %param.8), channel_id=1, replica_groups={{0,4,8,12},{1,5,9,13},{2,6,10,14},{3,7,11,15},{16,20,24,28},{17,21,25,2..., dimensions={0}, use_global_device_ids=true | all-gather | bytes 245760 | tf_op jit(solution)/shard_map/all_gather | solution.py:228
  35.2 1.4 copy-done.1
  36.6 2.0 act_grad_body.1
  38.6 3.5 %all-to-all-start.2 = ((bf16[4,1024,128]{2,1,0:T(8,128)(2,1)}), bf16[4,1024,128]{2,1,0:T(8,128)(2,1)S(1)}, u32[]{:S(2)}, u32[]{:S(2)}) async-start(bf16[4,1024,128]{2,1,0:T(8,128)(2,1)} %bitcast.10), calls=%async_computation.2 | async-start | bytes 2097152 | tf_op jit(solution)/shard_map/all_to_all | solution.py:204
  42.1 36.0 %all_gather.16 = bf16[1024,384]{1,0:T(8,128)(2,1)S(1)} all-gather(bf16[256,384]{1,0:T(8,128)(2,1)S(1)} %all_gather.15), channel_id=1, replica_groups={{0,1,2,3},{4,5,6,7},{8,9,10,11},{12,13,14,15},{16,17,18,19},{20,21,22,2..., dimensions={0}, use_global_device_ids=true | all-gather | bytes 983040 | tf_op jit(solution)/shard_map/all_gather | solution.py:228
  79.1 1.6 copy-done
  81.7 11.7 %all-to-all-start.1 = ((bf16[32,8,6144]{2,1,0:T(8,128)(2,1)}), bf16[32,8,6144]{2,1,0:T(8,128)(2,1)S(1)}, u32[]{:S(2)}, u32[]{:S(2)}) async-start(bf16[32,8,6144]{2,1,0:T(8,128)(2,1)} %bitcast.21), calls=%async_computation.1 | async-start | bytes 6291456 | tf_op jit(solution)/shard_map/all_to_all | solution.py:179
  93.4 1.2 copy-done.4
  94.7 3.6 %collective-permute-start = (bf16[256,128]{1,0:T(8,128)(2,1)S(1)}, bf16[256,128]{1,0:T(8,128)(2,1)S(1)}, u32[]{:S(2)}, u32[]{:S(2)}) collective-permute-start(bf16[256,128]{1,0:T(8,128)(2,1)S(1)} %get-tuple-element.30), channel_id=1, source_target_pairs={{0,4},{1,5},{2,6},{3,7},{4,8},{5,9},{6,10},{7,11},{8,12},{9,13},{1... | collective-permute-start | bytes 196616 | tf_op jit(solution)/shard_map/ppermute | solution.py:224
  98.3 7.0 %collective-permute-start.1 = (bf16[256,128]{1,0:T(8,128)(2,1)S(1)}, bf16[256,128]{1,0:T(8,128)(2,1)S(1)}, u32[]{:S(2)}, u32[]{:S(2)}) collective-permute-start(bf16[256,128]{1,0:T(8,128)(2,1)S(1)} %get-tuple-element.31), channel_id=1, source_target_pairs={{0,8},{1,9},{2,10},{3,11},{4,12},{5,13},{6,14},{7,15},{8,0},{9,1},... | collective-permute-start | bytes 196616 | tf_op jit(solution)/shard_map/ppermute | solution.py:224
  105.3 5.6 %collective-permute-start.2 = (bf16[256,128]{1,0:T(8,128)(2,1)S(1)}, bf16[256,128]{1,0:T(8,128)(2,1)S(1)}, u32[]{:S(2)}, u32[]{:S(2)}) collective-permute-start(bf16[256,128]{1,0:T(8,128)(2,1)S(1)} %get-tuple-element.32), channel_id=1, source_target_pairs={{0,12},{1,13},{2,14},{3,15},{4,0},{5,1},{6,2},{7,3},{8,4},{9,5},{1... | collective-permute-start | bytes 196616 | tf_op jit(solution)/shard_map/ppermute | solution.py:224
  110.9 1.9 collective-permute-done.1.refs_2_
  112.8 8.1 %collective-permute-done.2.refs_3_ = bf16[256,128]{1,0:T(8,128)(2,1)S(1)} collective-permute-done((bf16[256,128]{1,0:T(8,128)(2,1)S(1)}, bf16[256,128]{1,0:T(8,128)(2,1)S(1)}, u32[]{:S(2)}, u32[]{:S(2)}) %collective-permute-start.2) | collective-permute-done | bytes 65568 | tf_op jit(solution)/shard_map/ppermute | solution.py:224
  121.6 11.6 %all-to-all-done.1 = bf16[32,8,6144]{2,1,0:T(8,128)(2,1)S(1)} async-done(((bf16[32,8,6144]{2,1,0:T(8,128)(2,1)}), bf16[32,8,6144]{2,1,0:T(8,128)(2,1)S(1)}, u32[]{:S(2)}, u32[]{:S(2)}) %all-to-all-start.1) | async-done | bytes 3145760 | tf_op jit(solution)/shard_map/all_to_all | solution.py:179
  133.1 1.4 copy-done.8
  134.5 1.4 copy-done.9
  136.9 3.5 %expert_body.1 = (bf16[256,128]{1,0:T(8,128)(2,1)S(1)}, bf16[256,6144]{1,0:T(8,128)(2,1)S(1)}) custom-call(bf16[256,6144]{1,0:T(8,128)(2,1)S(1)} %bitcast.20, bf16[6144,128]{1,0:T(8,128)(2,1)S(1)} %copy-done.8, bf16[6144,128]{1,0:T(8,128)(2,1)S(1)} %copy-done.9, bf16[256,512]{1,0:T(8,128)(2,1)S(1)} %bitcast.29, f32[256,128]{1,0:T(8,128)S(1)} %copy-done.12), custom_call_target="tpu_custom_call" | custom-call | flops 1610612736 | bytes 9895936 | tf_op jit(solution)/shard_map/expert_body/pallas_call | solution.py:50
  140.3 1.6 copy-done.5
  142.0 5.0 %all-to-all-start.3 = ((bf16[32,8,6144]{2,1,0:T(8,128)(2,1)}), bf16[32,8,6144]{2,1,0:T(8,128)(2,1)S(1)}, u32[]{:S(2)}, u32[]{:S(2)}) async-start(bf16[32,8,6144]{2,1,0:T(8,128)(2,1)} %bitcast.24), calls=%async_computation.3 | async-start | bytes 6291456 | tf_op jit(solution)/shard_map/all_to_all | solution.py:179
  147.0 16.6 %all_gather.17 = bf16[1024,128]{1,0:T(8,128)(2,1)S(1)} all-gather(bf16[256,128]{1,0:T(8,128)(2,1)S(1)} %get-tuple-element.33), channel_id=1, replica_groups={{0,4,8,12},{1,5,9,13},{2,6,10,14},{3,7,11,15},{16,20,24,28},{17,21,25,2..., dimensions={0}, use_global_device_ids=true | all-gather | bytes 327680 | tf_op jit(solution)/shard_map/all_gather | solution.py:228
  164.2 16.3 %all_gather.18 = bf16[2048,128]{1,0:T(8,128)(2,1)} all-gather(bf16[512,128]{1,0:T(8,128)(2,1)S(1)} %get-tuple-element.48), channel_id=1, replica_groups={{0,1,2,3},{4,5,6,7},{8,9,10,11},{12,13,14,15},{16,17,18,19},{20,21,22,2..., dimensions={0}, use_global_device_ids=true | all-gather | bytes 655360 | tf_op jit(solution)/shard_map/all_gather | solution.py:228
  180.4 6.3 %all-to-all-done.3 = bf16[32,8,6144]{2,1,0:T(8,128)(2,1)S(1)} async-done(((bf16[32,8,6144]{2,1,0:T(8,128)(2,1)}), bf16[32,8,6144]{2,1,0:T(8,128)(2,1)S(1)}, u32[]{:S(2)}, u32[]{:S(2)}) %all-to-all-start.3) | async-done | bytes 3145760 | tf_op jit(solution)/shard_map/all_to_all | solution.py:179
  188.2 3.9 %all-to-all-start.4 = ((bf16[4,256,384]{2,1,0:T(8,128)(2,1)}), bf16[4,256,384]{2,1,0:T(8,128)(2,1)S(1)}, u32[]{:S(2)}, u32[]{:S(2)}) async-start(bf16[4,256,384]{2,1,0:T(8,128)(2,1)} %bitcast.26), calls=%async_computation.4 | async-start | bytes 1572864 | tf_op jit(solution)/shard_map/all_to_all | solution.py:204
  192.1 27.5 %all_gather.19 = bf16[2048,128]{1,0:T(8,128)(2,1)S(1)} all-gather(bf16[512,128]{1,0:T(8,128)(2,1)S(1)} %copy-done.13), channel_id=1, replica_groups={{0,1,2,3},{4,5,6,7},{8,9,10,11},{12,13,14,15},{16,17,18,19},{20,21,22,2..., dimensions={0}, use_global_device_ids=true | all-gather | bytes 655360 | tf_op jit(solution)/shard_map/all_gather | solution.py:228
  220.6 1.4 down_body.1
  222.1 7.4 %all-to-all-start.5 = ((bf16[32,8,384]{2,1,0:T(8,128)(2,1)}), bf16[32,8,384]{2,1,0:T(8,128)(2,1)S(1)}, u32[]{:S(2)}, u32[]{:S(2)}) async-start(bf16[32,8,384]{2,1,0:T(8,128)(2,1)} %bitcast.18), calls=%async_computation.5 | async-start | bytes 393216 | tf_op jit(solution)/shard_map/all_to_all | solution.py:179
  229.5 3.8 %collective-permute-start.3 = (bf16[64,384]{1,0:T(8,128)(2,1)S(1)}, bf16[64,384]{1,0:T(8,128)(2,1)S(1)}, u32[]{:S(2)}, u32[]{:S(2)}) collective-permute-start(bf16[64,384]{1,0:T(8,128)(2,1)S(1)} %get-tuple-element.45), channel_id=1, source_target_pairs={{0,4},{1,5},{2,6},{3,7},{4,8},{5,9},{6,10},{7,11},{8,12},{9,13},{1... | collective-permute-start | bytes 147464 | tf_op jit(solution)/shard_map/ppermute | solution.py:224
  233.3 7.0 %collective-permute-start.4 = (bf16[64,384]{1,0:T(8,128)(2,1)S(1)}, bf16[64,384]{1,0:T(8,128)(2,1)S(1)}, u32[]{:S(2)}, u32[]{:S(2)}) collective-permute-start(bf16[64,384]{1,0:T(8,128)(2,1)S(1)} %get-tuple-element.46), channel_id=1, source_target_pairs={{0,8},{1,9},{2,10},{3,11},{4,12},{5,13},{6,14},{7,15},{8,0},{9,1},... | collective-permute-start | bytes 147464 | tf_op jit(solution)/shard_map/ppermute | solution.py:224
  240.3 5.4 %collective-permute-start.5 = (bf16[64,384]{1,0:T(8,128)(2,1)S(1)}, bf16[64,384]{1,0:T(8,128)(2,1)S(1)}, u32[]{:S(2)}, u32[]{:S(2)}) collective-permute-start(bf16[64,384]{1,0:T(8,128)(2,1)S(1)} %get-tuple-element.47), channel_id=1, source_target_pairs={{0,12},{1,13},{2,14},{3,15},{4,0},{5,1},{6,2},{7,3},{8,4},{9,5},{1... | collective-permute-start | bytes 147464 | tf_op jit(solution)/shard_map/ppermute | solution.py:224
  247.0 7.3 %collective-permute-done.5.refs_3_ = bf16[64,384]{1,0:T(8,128)(2,1)S(1)} collective-permute-done((bf16[64,384]{1,0:T(8,128)(2,1)S(1)}, bf16[64,384]{1,0:T(8,128)(2,1)S(1)}, u32[]{:S(2)}, u32[]{:S(2)}) %collective-permute-start.5) | collective-permute-done | bytes 49184 | tf_op jit(solution)/shard_map/ppermute | solution.py:224
  (37 shorter events, 9.6 us)
Async XLA Ops:
  2.6 32.6 %all-to-all-start = ((bf16[32,8,512]{2,1,0:T(8,128)(2,1)}), bf16[32,8,512]{2,1,0:T(8,128)(2,1)S(1)}, u32[]{:S(2)}, u32[]{:S(2)}) async-start(bf16[32,8,512]{2,1,0:T(8,128)(2,1)} %bitcast.33), calls=%async_computation | async-start | bytes 524288 | tf_op jit(solution)/shard_map/all_to_all | solution.py:179
  13.0 65.1 %copy-start.10 = (bf16[256,64]{1,0:T(8,128)(2,1)S(1)}, bf16[256,64]{1,0:T(8,128)(2,1)}, u32[]{:S(2)}) copy-start(bf16[256,64]{1,0:T(8,128)(2,1)} %get-tuple-element.25.refs_0_) | copy-start | bytes 98308
  35.2 1.4 copy-start.1
  38.6 42.2 %all-to-all-start.2 = ((bf16[4,1024,128]{2,1,0:T(8,128)(2,1)}), bf16[4,1024,128]{2,1,0:T(8,128)(2,1)S(1)}, u32[]{:S(2)}, u32[]{:S(2)}) async-start(bf16[4,1024,128]{2,1,0:T(8,128)(2,1)} %bitcast.10), calls=%async_computation.2 | async-start | bytes 2097152 | tf_op jit(solution)/shard_map/all_to_all | solution.py:204
  79.1 1.6 copy-start
  80.7 1.0 copy-start.3
  81.7 51.4 %all-to-all-start.1 = ((bf16[32,8,6144]{2,1,0:T(8,128)(2,1)}), bf16[32,8,6144]{2,1,0:T(8,128)(2,1)S(1)}, u32[]{:S(2)}, u32[]{:S(2)}) async-start(bf16[32,8,6144]{2,1,0:T(8,128)(2,1)} %bitcast.21), calls=%async_computation.1 | async-start | bytes 6291456 | tf_op jit(solution)/shard_map/all_to_all | solution.py:179
  93.4 1.2 copy-start.4
  94.7 16.1 %collective-permute-start = (bf16[256,128]{1,0:T(8,128)(2,1)S(1)}, bf16[256,128]{1,0:T(8,128)(2,1)S(1)}, u32[]{:S(2)}, u32[]{:S(2)}) collective-permute-start(bf16[256,128]{1,0:T(8,128)(2,1)S(1)} %get-tuple-element.30), channel_id=1, source_target_pairs={{0,4},{1,5},{2,6},{3,7},{4,8},{5,9},{6,10},{7,11},{8,12},{9,13},{1... | collective-permute-start | bytes 196616 | tf_op jit(solution)/shard_map/ppermute | solution.py:224
  98.3 14.4 %collective-permute-start.1 = (bf16[256,128]{1,0:T(8,128)(2,1)S(1)}, bf16[256,128]{1,0:T(8,128)(2,1)S(1)}, u32[]{:S(2)}, u32[]{:S(2)}) collective-permute-start(bf16[256,128]{1,0:T(8,128)(2,1)S(1)} %get-tuple-element.31), channel_id=1, source_target_pairs={{0,8},{1,9},{2,10},{3,11},{4,12},{5,13},{6,14},{7,15},{8,0},{9,1},... | collective-permute-start | bytes 196616 | tf_op jit(solution)/shard_map/ppermute | solution.py:224
  105.3 15.5 %collective-permute-start.2 = (bf16[256,128]{1,0:T(8,128)(2,1)S(1)}, bf16[256,128]{1,0:T(8,128)(2,1)S(1)}, u32[]{:S(2)}, u32[]{:S(2)}) collective-permute-start(bf16[256,128]{1,0:T(8,128)(2,1)S(1)} %get-tuple-element.32), channel_id=1, source_target_pairs={{0,12},{1,13},{2,14},{3,15},{4,0},{5,1},{6,2},{7,3},{8,4},{9,5},{1... | collective-permute-start | bytes 196616 | tf_op jit(solution)/shard_map/ppermute | solution.py:224
  120.9 0.7 copy-start.11
  133.1 1.4 copy-start.8
  134.5 1.4 copy-start.9
  136.0 0.9 copy-start.12
  140.3 1.6 copy-start.5
  142.0 44.8 %all-to-all-start.3 = ((bf16[32,8,6144]{2,1,0:T(8,128)(2,1)}), bf16[32,8,6144]{2,1,0:T(8,128)(2,1)S(1)}, u32[]{:S(2)}, u32[]{:S(2)}) async-start(bf16[32,8,6144]{2,1,0:T(8,128)(2,1)} %bitcast.24), calls=%async_computation.3 | async-start | bytes 6291456 | tf_op jit(solution)/shard_map/all_to_all | solution.py:179
  164.2 27.9 %copy-start.13 = (bf16[512,128]{1,0:T(8,128)(2,1)S(1)}, bf16[512,128]{1,0:T(8,128)(2,1)}, u32[]{:S(2)}) copy-start(bf16[512,128]{1,0:T(8,128)(2,1)} %get-tuple-element.42) | copy-start | bytes 393220
  187.3 0.9 copy-start.6
  188.2 31.4 %copy-start.2 = (bf16[2048,384]{1,0:T(8,128)(2,1)S(1)}, bf16[2048,384]{1,0:T(8,128)(2,1)}, u32[]{:S(2)}) copy-start(bf16[2048,384]{1,0:T(8,128)(2,1)} %refs_2_.3) | copy-start | bytes 4718596
  188.2 33.8 %all-to-all-start.4 = ((bf16[4,256,384]{2,1,0:T(8,128)(2,1)}), bf16[4,256,384]{2,1,0:T(8,128)(2,1)S(1)}, u32[]{:S(2)}, u32[]{:S(2)}) async-start(bf16[4,256,384]{2,1,0:T(8,128)(2,1)} %bitcast.26), calls=%async_computation.4 | async-start | bytes 1572864 | tf_op jit(solution)/shard_map/all_to_all | solution.py:204
  219.6 1.0 copy-start.7
  222.1 32.8 %all-to-all-start.5 = ((bf16[32,8,384]{2,1,0:T(8,128)(2,1)}), bf16[32,8,384]{2,1,0:T(8,128)(2,1)S(1)}, u32[]{:S(2)}, u32[]{:S(2)}) async-start(bf16[32,8,384]{2,1,0:T(8,128)(2,1)} %bitcast.18), calls=%async_computation.5 | async-start | bytes 393216 | tf_op jit(solution)/shard_map/all_to_all | solution.py:179
  229.5 16.2 %collective-permute-start.3 = (bf16[64,384]{1,0:T(8,128)(2,1)S(1)}, bf16[64,384]{1,0:T(8,128)(2,1)S(1)}, u32[]{:S(2)}, u32[]{:S(2)}) collective-permute-start(bf16[64,384]{1,0:T(8,128)(2,1)S(1)} %get-tuple-element.45), channel_id=1, source_target_pairs={{0,4},{1,5},{2,6},{3,7},{4,8},{5,9},{6,10},{7,11},{8,12},{9,13},{1... | collective-permute-start | bytes 147464 | tf_op jit(solution)/shard_map/ppermute | solution.py:224
  233.3 13.7 %collective-permute-start.4 = (bf16[64,384]{1,0:T(8,128)(2,1)S(1)}, bf16[64,384]{1,0:T(8,128)(2,1)S(1)}, u32[]{:S(2)}, u32[]{:S(2)}) collective-permute-start(bf16[64,384]{1,0:T(8,128)(2,1)S(1)} %get-tuple-element.46), channel_id=1, source_target_pairs={{0,8},{1,9},{2,10},{3,11},{4,12},{5,13},{6,14},{7,15},{8,0},{9,1},... | collective-permute-start | bytes 147464 | tf_op jit(solution)/shard_map/ppermute | solution.py:224
  240.3 14.0 %collective-permute-start.5 = (bf16[64,384]{1,0:T(8,128)(2,1)S(1)}, bf16[64,384]{1,0:T(8,128)(2,1)S(1)}, u32[]{:S(2)}, u32[]{:S(2)}) collective-permute-start(bf16[64,384]{1,0:T(8,128)(2,1)S(1)} %get-tuple-element.47), channel_id=1, source_target_pairs={{0,12},{1,13},{2,14},{3,15},{4,0},{5,1},{6,2},{7,3},{8,4},{9,5},{1... | collective-permute-start | bytes 147464 | tf_op jit(solution)/shard_map/ppermute | solution.py:224
